TPU v7x, 1024 devices: a whole 4x4x32 slice. The times are simulated.
1024 devices in a mesh: gr: 128 (over z_lo, y, core), gc: 8 (over x, z_hi).
Axes of the slice: x: 4, y: 4, z: 32 (z_hi: 2, z_lo: 16; z = z_hi * 16 + z_lo), core: 2. Of those that a mesh axis runs over, the one named last changes fastest.
Arguments:
- density: float32 [1024, 9, 128, 128], P(('gr', 'gc')), as said below
- reach: int32 [1024], replicated, may hold values from 1 to 4, as said below
Outputs:
- purified: float32 [1024, 9, 128, 128], P(('gr', 'gc'))
Inputs may be any that keep to these rules, and one draw needn't show every extreme that they name: Every 16th block row, from row 0, has reach 4. `density`: Symmetric: block (i, i + d) is the transpose of block (i + d, i); blocks outside the pattern given by reach are zero.
All inputs are finite; a program needn't handle non-finite values.
Results may differ from a plain program's by a relative error of at most 0.022.
Values sent between devices are 32-bit elements; how exact they have to be, the bound alone decides.
A program may use at most 64 MiB of HBM per device.

v0:
```python
import jax
import jax.numpy as jnp
from jax import lax
from jax.sharding import PartitionSpec as P

STEPS = 2


def from_behind(block, axis, distance):
    devices = range(lax.axis_size(axis))
    route = [((i - distance) % len(devices), i) for i in devices]
    return lax.ppermute(block, axis, route)


def place_piece(piece, offset):
    if offset > 0:
        return jnp.pad(piece, ((offset, 0), (0, 0), (0, 0)))
    return jnp.pad(piece, ((0, -offset), (0, 0), (0, 0)))


def full_layers(band_row, pieces, half):
    layers = []
    for offset in range(-half, half + 1):
        if offset == 0:
            layers.append(band_row)
        else:
            layers.append(place_piece(pieces[offset], offset))
    return jnp.stack(layers, axis=0)


def neighbour_window(band_row):
    width = band_row.shape[0]
    half = (width - 1) // 2
    pieces = {}
    signed = [s for hop in range(1, half + 1) for s in (hop, -hop)]
    for offset in signed:
        sent = band_row[max(0, -offset) : min(width, width - offset)]
        pieces[offset] = from_behind(sent, ("gr", "gc"), -offset)
    return full_layers(band_row, pieces, half)


def local(density, reach):
    band_row = density[0]
    width = band_row.shape[0]
    half = (width - 1) // 2
    total = reach.shape[0]
    position = lax.axis_index(("gr", "gc"))
    offsets = jnp.arange(-half, half + 1, dtype=jnp.int32)
    nearby = jnp.take(reach, (position + offsets) % total)
    own_reach = jnp.take(reach, position)
    keep = (jnp.abs(offsets) <= jnp.minimum(own_reach, nearby)).astype(jnp.float32)[:, None, None]
    for sweep in range(STEPS):
        window = neighbour_window(band_row)
        square = (
            jnp.einsum("eab,edbc->dac", band_row, window, precision=lax.Precision.HIGHEST) * keep
        )
        cube = jnp.einsum("eab,edbc->dac", square, window, precision=lax.Precision.HIGHEST) * keep
        band_row = 3.0 * square - 2.0 * cube
    return band_row[None]


def solution(mesh):
    placed = (P(("gr", "gc"), None, None, None), P())
    return jax.shard_map(
        local,
        mesh=mesh,
        in_specs=placed,
        out_specs=P(("gr", "gc"), None, None, None),
        check_vma=False,
    )
```

profile of v0, /device:TPU:409, one launch (start us, length us, event | category | flops | bytes accessed | tf_op | source)
XLA Modules:
  0.0 871.0 jit_solution(6032450806314642620)
XLA Ops:
  2.1 4.8 collective-permute-start
  9.0 14.3 %collective-permute-start.1 = (f32[6,128,128]{1,2,0:T(8,128)}, f32[6,128,128]{1,2,0:T(8,128)}, u32[]{:S(2)}, u32[]{:S(2)}) collective-permute-start(f32[6,128,128]{1,2,0:T(8,128)} %bitcast.2), channel_id=1, source_target_pairs={{1021,0},{1022,1},{1023,2},{0,3},{1,4},{2,5},{3,6},{4,7},{5,8},{6,... | collective-permute-start | bytes 1179656 | tf_op jit(solution)/shard_map/ppermute | solution.py:12
  25.4 2.2 collective-permute-start.2
  28.7 11.8 %collective-permute-start.3 = (f32[8,128,128]{1,2,0:T(8,128)}, f32[8,128,128]{1,2,0:T(8,128)}, u32[]{:S(2)}, u32[]{:S(2)}) collective-permute-start(f32[8,128,128]{1,2,0:T(8,128)} %bitcast.6), channel_id=1, source_target_pairs={{1023,0},{0,1},{1,2},{2,3},{3,4},{4,5},{5,6},{6,7},{7,8},{8,9},{9,... | collective-permute-start | bytes 1572872 | tf_op jit(solution)/shard_map/ppermute | solution.py:12
  40.7 14.2 %collective-permute-start.4 = (f32[8,128,128]{1,2,0:T(8,128)S(1)}, f32[8,128,128]{1,2,0:T(8,128)}, u32[]{:S(2)}, u32[]{:S(2)}) collective-permute-start(f32[8,128,128]{1,2,0:T(8,128)S(1)} %bitcast.121), channel_id=1, source_target_pairs={{1,0},{2,1},{3,2},{4,3},{5,4},{6,5},{7,6},{8,7},{9,8},{10,9},{11,1... | collective-permute-start | bytes 1572872 | tf_op jit(solution)/shard_map/ppermute | solution.py:12
  59.2 3.7 collective-permute-start.5
  63.9 46.8 %collective-permute-done.1 = f32[6,128,128]{1,2,0:T(8,128)} collective-permute-done((f32[6,128,128]{1,2,0:T(8,128)}, f32[6,128,128]{1,2,0:T(8,128)}, u32[]{:S(2)}, u32[]{:S(2)}) %collective-permute-start.1) | collective-permute-done | bytes 393248 | tf_op jit(solution)/shard_map/ppermute | solution.py:12
  113.9 27.1 %collective-permute-start.7 = (f32[5,128,128]{1,2,0:T(8,128)}, f32[5,128,128]{1,2,0:T(8,128)S(1)}, u32[]{:S(2)}, u32[]{:S(2)}) collective-permute-start(f32[5,128,128]{1,2,0:T(8,128)} %bitcast.124), channel_id=1, source_target_pairs={{4,0},{5,1},{6,2},{7,3},{8,4},{9,5},{10,6},{11,7},{12,8},{13,9},{1... | collective-permute-start | bytes 983048 | tf_op jit(solution)/shard_map/ppermute | solution.py:12
  142.1 31.1 %collective-permute-done.3 = f32[8,128,128]{1,2,0:T(8,128)} collective-permute-done((f32[8,128,128]{1,2,0:T(8,128)}, f32[8,128,128]{1,2,0:T(8,128)}, u32[]{:S(2)}, u32[]{:S(2)}) %collective-permute-start.3) | collective-permute-done | bytes 524320 | tf_op jit(solution)/shard_map/ppermute | solution.py:12
  174.3 125.5 %collective-permute-done.4 = f32[8,128,128]{1,2,0:T(8,128)} collective-permute-done((f32[8,128,128]{1,2,0:T(8,128)S(1)}, f32[8,128,128]{1,2,0:T(8,128)}, u32[]{:S(2)}, u32[]{:S(2)}) %collective-permute-start.4) | collective-permute-done | bytes 524320 | tf_op jit(solution)/shard_map/ppermute | solution.py:12
  301.0 13.2 %collective-permute-done.6 = f32[6,128,128]{1,2,0:T(8,128)S(1)} collective-permute-done((f32[6,128,128]{1,2,0:T(8,128)}, f32[6,128,128]{1,2,0:T(8,128)S(1)}, u32[]{:S(2)}, u32[]{:S(2)}) %collective-permute-start.6) | collective-permute-done | bytes 393248 | tf_op jit(solution)/shard_map/ppermute | solution.py:12
  314.3 4.5 fusion.3
  318.8 4.5 fusion.6
  323.5 47.1 %collective-permute-start.8 = (f32[5,128,128]{1,2,0:T(8,128)S(1)}, f32[5,128,128]{1,2,0:T(8,128)S(1)}, u32[]{:S(2)}, u32[]{:S(2)}) collective-permute-start(f32[5,128,128]{1,2,0:T(8,128)S(1)} %get-tuple-element.17), channel_id=1, source_target_pairs={{1020,0},{1021,1},{1022,2},{1023,3},{0,4},{1,5},{2,6},{3,7},{4,8},... | collective-permute-start | bytes 983048 | tf_op jit(solution)/shard_map/ppermute | solution.py:12
  370.6 188.4 %collective-permute-start.9 = (f32[6,128,128]{1,2,0:T(8,128)S(1)}, f32[6,128,128]{1,2,0:T(8,128)S(1)}, u32[]{:S(2)}, u32[]{:S(2)}) collective-permute-start(f32[6,128,128]{1,2,0:T(8,128)S(1)} %get-tuple-element.19), channel_id=1, source_target_pairs={{1021,0},{1022,1},{1023,2},{0,3},{1,4},{2,5},{3,6},{4,7},{5,8},{6,... | collective-permute-start | bytes 1179656 | tf_op jit(solution)/shard_map/ppermute | solution.py:12
  559.0 243.6 %collective-permute-start.10 = (f32[7,128,128]{1,2,0:T(8,128)S(1)}, f32[7,128,128]{1,2,0:T(8,128)S(1)}, u32[]{:S(2)}, u32[]{:S(2)}) collective-permute-start(f32[7,128,128]{1,2,0:T(8,128)S(1)} %get-tuple-element.21), channel_id=1, source_target_pairs={{1022,0},{1023,1},{0,2},{1,3},{2,4},{3,5},{4,6},{5,7},{6,8},{7,9},... | collective-permute-start | bytes 1376264 | tf_op jit(solution)/shard_map/ppermute | solution.py:12
  802.7 3.1 collective-permute-start.11
  805.8 22.9 %collective-permute-start.12 = (f32[8,128,128]{1,2,0:T(8,128)S(1)}, f32[8,128,128]{1,2,0:T(8,128)S(1)}, u32[]{:S(2)}, u32[]{:S(2)}) collective-permute-start(f32[8,128,128]{1,2,0:T(8,128)S(1)} %get-tuple-element.22), channel_id=1, source_target_pairs={{1,0},{2,1},{3,2},{4,3},{5,4},{6,5},{7,6},{8,7},{9,8},{10,9},{11,1... | collective-permute-start | bytes 1572872 | tf_op jit(solution)/shard_map/ppermute | solution.py:12
  828.7 4.3 collective-permute-start.13
  833.0 3.4 collective-permute-start.14
  836.5 2.1 collective-permute-start.15
  838.9 21.9 %collective-permute-done.14 = f32[6,128,128]{1,2,0:T(8,128)S(1)} collective-permute-done((f32[6,128,128]{1,2,0:T(8,128)S(1)}, f32[6,128,128]{1,2,0:T(8,128)S(1)}, u32[]{:S(2)}, u32[]{:S(2)}) %collective-permute-start.14) | collective-permute-done | bytes 393248 | tf_op jit(solution)/shard_map/ppermute | solution.py:12
  860.9 4.5 fusion.1
  865.4 4.5 fusion.10
  (57 shorter events, 20.4 us)
Async XLA Ops:
  0.0 27.6 %copy-start.1 = (f32[1,9,128,128]{3,2,1,0:T(8,128)S(1)}, f32[1,9,128,128]{3,2,1,0:T(8,128)}, u32[]{:S(2)}) copy-start(f32[1,9,128,128]{3,2,1,0:T(8,128)} %param.2) | copy-start | bytes 1769476
  2.1 53.1 %copy-start = (s32[1024]{0:T(1024)S(1)}, s32[1024]{0:T(1024)}, u32[]{:S(2)}) copy-start(s32[1024]{0:T(1024)} %param.3) | copy-start | bytes 12292
  2.1 57.1 %collective-permute-start = (f32[5,128,128]{1,2,0:T(8,128)}, f32[5,128,128]{1,2,0:T(8,128)}, u32[]{:S(2)}, u32[]{:S(2)}) collective-permute-start(f32[5,128,128]{1,2,0:T(8,128)} %bitcast), channel_id=1, source_target_pairs={{1020,0},{1021,1},{1022,2},{1023,3},{0,4},{1,5},{2,6},{3,7},{4,8},... | collective-permute-start | bytes 983048 | tf_op jit(solution)/shard_map/ppermute | solution.py:12
  9.0 101.8 %collective-permute-start.1 = (f32[6,128,128]{1,2,0:T(8,128)}, f32[6,128,128]{1,2,0:T(8,128)}, u32[]{:S(2)}, u32[]{:S(2)}) collective-permute-start(f32[6,128,128]{1,2,0:T(8,128)} %bitcast.2), channel_id=1, source_target_pairs={{1021,0},{1022,1},{1023,2},{0,3},{1,4},{2,5},{3,6},{4,7},{5,8},{6,... | collective-permute-start | bytes 1179656 | tf_op jit(solution)/shard_map/ppermute | solution.py:12
  25.4 88.4 %collective-permute-start.2 = (f32[7,128,128]{1,2,0:T(8,128)}, f32[7,128,128]{1,2,0:T(8,128)}, u32[]{:S(2)}, u32[]{:S(2)}) collective-permute-start(f32[7,128,128]{1,2,0:T(8,128)} %bitcast.4), channel_id=1, source_target_pairs={{1022,0},{1023,1},{0,2},{1,3},{2,4},{3,5},{4,6},{5,7},{6,8},{7,9},... | collective-permute-start | bytes 1376264 | tf_op jit(solution)/shard_map/ppermute | solution.py:12
  28.7 144.5 %collective-permute-start.3 = (f32[8,128,128]{1,2,0:T(8,128)}, f32[8,128,128]{1,2,0:T(8,128)}, u32[]{:S(2)}, u32[]{:S(2)}) collective-permute-start(f32[8,128,128]{1,2,0:T(8,128)} %bitcast.6), channel_id=1, source_target_pairs={{1023,0},{0,1},{1,2},{2,3},{3,4},{4,5},{5,6},{6,7},{7,8},{8,9},{9,... | collective-permute-start | bytes 1572872 | tf_op jit(solution)/shard_map/ppermute | solution.py:12
  40.7 259.2 %collective-permute-start.4 = (f32[8,128,128]{1,2,0:T(8,128)S(1)}, f32[8,128,128]{1,2,0:T(8,128)}, u32[]{:S(2)}, u32[]{:S(2)}) collective-permute-start(f32[8,128,128]{1,2,0:T(8,128)S(1)} %bitcast.121), channel_id=1, source_target_pairs={{1,0},{2,1},{3,2},{4,3},{5,4},{6,5},{7,6},{8,7},{9,8},{10,9},{11,1... | collective-permute-start | bytes 1572872 | tf_op jit(solution)/shard_map/ppermute | solution.py:12
  59.2 241.7 %collective-permute-start.5 = (f32[7,128,128]{1,2,0:T(8,128)S(1)}, f32[7,128,128]{1,2,0:T(8,128)S(1)}, u32[]{:S(2)}, u32[]{:S(2)}) collective-permute-start(f32[7,128,128]{1,2,0:T(8,128)S(1)} %bitcast.122), channel_id=1, source_target_pairs={{2,0},{3,1},{4,2},{5,3},{6,4},{7,5},{8,6},{9,7},{10,8},{11,9},{12,... | collective-permute-start | bytes 1376264 | tf_op jit(solution)/shard_map/ppermute | solution.py:12
  110.7 203.4 %collective-permute-start.6 = (f32[6,128,128]{1,2,0:T(8,128)}, f32[6,128,128]{1,2,0:T(8,128)S(1)}, u32[]{:S(2)}, u32[]{:S(2)}) collective-permute-start(f32[6,128,128]{1,2,0:T(8,128)} %bitcast.123), channel_id=1, source_target_pairs={{3,0},{4,1},{5,2},{6,3},{7,4},{8,5},{9,6},{10,7},{11,8},{12,9},{13... | collective-permute-start | bytes 1179656 | tf_op jit(solution)/shard_map/ppermute | solution.py:12
  113.9 200.3 %collective-permute-start.7 = (f32[5,128,128]{1,2,0:T(8,128)}, f32[5,128,128]{1,2,0:T(8,128)S(1)}, u32[]{:S(2)}, u32[]{:S(2)}) collective-permute-start(f32[5,128,128]{1,2,0:T(8,128)} %bitcast.124), channel_id=1, source_target_pairs={{4,0},{5,1},{6,2},{7,3},{8,4},{9,5},{10,6},{11,7},{12,8},{13,9},{1... | collective-permute-start | bytes 983048 | tf_op jit(solution)/shard_map/ppermute | solution.py:12
  323.5 505.2 %collective-permute-start.8 = (f32[5,128,128]{1,2,0:T(8,128)S(1)}, f32[5,128,128]{1,2,0:T(8,128)S(1)}, u32[]{:S(2)}, u32[]{:S(2)}) collective-permute-start(f32[5,128,128]{1,2,0:T(8,128)S(1)} %get-tuple-element.17), channel_id=1, source_target_pairs={{1020,0},{1021,1},{1022,2},{1023,3},{0,4},{1,5},{2,6},{3,7},{4,8},... | collective-permute-start | bytes 983048 | tf_op jit(solution)/shard_map/ppermute | solution.py:12
  370.6 462.4 %collective-permute-start.9 = (f32[6,128,128]{1,2,0:T(8,128)S(1)}, f32[6,128,128]{1,2,0:T(8,128)S(1)}, u32[]{:S(2)}, u32[]{:S(2)}) collective-permute-start(f32[6,128,128]{1,2,0:T(8,128)S(1)} %get-tuple-element.19), channel_id=1, source_target_pairs={{1021,0},{1022,1},{1023,2},{0,3},{1,4},{2,5},{3,6},{4,7},{5,8},{6,... | collective-permute-start | bytes 1179656 | tf_op jit(solution)/shard_map/ppermute | solution.py:12
  559.0 277.4 %collective-permute-start.10 = (f32[7,128,128]{1,2,0:T(8,128)S(1)}, f32[7,128,128]{1,2,0:T(8,128)S(1)}, u32[]{:S(2)}, u32[]{:S(2)}) collective-permute-start(f32[7,128,128]{1,2,0:T(8,128)S(1)} %get-tuple-element.21), channel_id=1, source_target_pairs={{1022,0},{1023,1},{0,2},{1,3},{2,4},{3,5},{4,6},{5,7},{6,8},{7,9},... | collective-permute-start | bytes 1376264 | tf_op jit(solution)/shard_map/ppermute | solution.py:12
  802.7 36.0 %collective-permute-start.11 = (f32[8,128,128]{1,2,0:T(8,128)S(1)}, f32[8,128,128]{1,2,0:T(8,128)S(1)}, u32[]{:S(2)}, u32[]{:S(2)}) collective-permute-start(f32[8,128,128]{1,2,0:T(8,128)S(1)} %get-tuple-element.23), channel_id=1, source_target_pairs={{1023,0},{0,1},{1,2},{2,3},{3,4},{4,5},{5,6},{6,7},{7,8},{8,9},{9,... | collective-permute-start | bytes 1572872 | tf_op jit(solution)/shard_map/ppermute | solution.py:12
  805.8 32.9 %collective-permute-start.12 = (f32[8,128,128]{1,2,0:T(8,128)S(1)}, f32[8,128,128]{1,2,0:T(8,128)S(1)}, u32[]{:S(2)}, u32[]{:S(2)}) collective-permute-start(f32[8,128,128]{1,2,0:T(8,128)S(1)} %get-tuple-element.22), channel_id=1, source_target_pairs={{1,0},{2,1},{3,2},{4,3},{5,4},{6,5},{7,6},{8,7},{9,8},{10,9},{11,1... | collective-permute-start | bytes 1572872 | tf_op jit(solution)/shard_map/ppermute | solution.py:12
  828.7 10.1 %collective-permute-start.13 = (f32[7,128,128]{1,2,0:T(8,128)S(1)}, f32[7,128,128]{1,2,0:T(8,128)S(1)}, u32[]{:S(2)}, u32[]{:S(2)}) collective-permute-start(f32[7,128,128]{1,2,0:T(8,128)S(1)} %get-tuple-element.20), channel_id=1, source_target_pairs={{2,0},{3,1},{4,2},{5,3},{6,4},{7,5},{8,6},{9,7},{10,8},{11,9},{12,... | collective-permute-start | bytes 1376264 | tf_op jit(solution)/shard_map/ppermute | solution.py:12
  833.0 27.7 %collective-permute-start.14 = (f32[6,128,128]{1,2,0:T(8,128)S(1)}, f32[6,128,128]{1,2,0:T(8,128)S(1)}, u32[]{:S(2)}, u32[]{:S(2)}) collective-permute-start(f32[6,128,128]{1,2,0:T(8,128)S(1)} %get-tuple-element.18), channel_id=1, source_target_pairs={{3,0},{4,1},{5,2},{6,3},{7,4},{8,5},{9,6},{10,7},{11,8},{12,9},{13... | collective-permute-start | bytes 1179656 | tf_op jit(solution)/shard_map/ppermute | solution.py:12
  836.5 24.4 %collective-permute-start.15 = (f32[5,128,128]{1,2,0:T(8,128)S(1)}, f32[5,128,128]{1,2,0:T(8,128)S(1)}, u32[]{:S(2)}, u32[]{:S(2)}) collective-permute-start(f32[5,128,128]{1,2,0:T(8,128)S(1)} %get-tuple-element.16), channel_id=1, source_target_pairs={{4,0},{5,1},{6,2},{7,3},{8,4},{9,5},{10,6},{11,7},{12,8},{13,9},{1... | collective-permute-start | bytes 983048 | tf_op jit(solution)/shard_map/ppermute | solution.py:12
where the time goes:
time: 873 us; the launch traced here: 871 us
  starting transfers between devices  595 us (68%)
  waiting for transfers between devices  239 us (27%)
  local copies, waits for them, and re-layouts  18.2 us (2%)
  matrix products  18 us (2%)
    ppermute x16, starting transfers between devices, from_behind(): return lax.ppermute(block, axis, route)  595 us
    ppermute x16, waiting for transfers between devices, from_behind(): return lax.ppermute(block, axis, route)  239 us
  transfers between devices with their start and end apart: 16, of which 5 were waited for; matrix products, arithmetic and copies ran while one was open for 2% of the time, Pallas kernels for 0%

commit v1 on v0

v1 whole, which is shorter than its diff:
```python
import jax
import jax.numpy as jnp
from jax import lax
from jax.experimental import pallas as pl
from jax.experimental.pallas import tpu as pltpu
from jax.sharding import PartitionSpec as P

MESH = pl.DeviceIdType.MESH
BS = 128
G = 2 * BS
F32 = jnp.float32
BF16 = jnp.bfloat16
NT = (((1,), (1,)), ((), ()))
NN = (((1,), (0,)), ((), ()))


def exchange(lines, x_ref, own, par, ssem, rsem, lsem):
    gr, gc = lax.axis_index("gr"), lax.axis_index("gc")
    x, s = gc // 2, lax.rem(gc, 2)
    sg = 1 - 2 * s
    up = (lax.rem(gr + 1, lines), gc)
    down = (lax.rem(gr + lines - 1, lines), gc)
    partner_gc = gc + sg
    partner = (gr, partner_gc)
    across_up = (up[0], partner_gc)
    across_down = (down[0], partner_gc)
    last, first = gr == lines - 1, gr == 0
    others = [lax.rem(x + step, 4) for step in (1, 3, 2)]
    peers = [(gr, o * 2 + s) for o in others]

    barrier = pltpu.get_barrier_semaphore()
    for d in [partner, up, down] + peers:
        pl.semaphore_signal(barrier, inc=1, device_id=d, device_id_type=MESH)

    @pl.when(last)
    def _():
        pl.semaphore_signal(barrier, inc=1, device_id=across_up, device_id_type=MESH)

    @pl.when(first)
    def _():
        pl.semaphore_signal(barrier, inc=1, device_id=across_down, device_id_type=MESH)

    extra = jnp.where(last, 1, 0) + jnp.where(first, 1, 0)
    pl.semaphore_wait(barrier, 6 + extra)

    count = [0]
    pending = []

    def copy(src, dst, device, k=None):
        if k is None:
            k = count[0]
            count[0] += 1
        return pltpu.make_async_remote_copy(src, dst, ssem.at[k], rsem.at[k], device_id=device, device_id_type=MESH)

    def send(src, dst, device):
        c = copy(src, dst, device)
        c.start()
        pending.append(c)
        return c

    wide = pl.ds(3 - 3 * s, 6)
    far = 4 - 3 * sg
    w6 = pl.ds(0, 6)
    slot_up, slot_down = 4 - 4 * sg, 4 + 4 * sg

    cross = [send(x_ref.at[0, 4 - 2 * n * sg], par.at[4, n], partner) for n in range(3)]
    edge_up, edge_down = [], []
    for n in range(3):
        k_up, k_down = count[0], count[0] + 1
        count[0] += 2
        edge_up.append(k_up)
        edge_down.append(k_down)

        @pl.when(last)
        def _():
            copy(x_ref.at[0, 4 - 2 * n * sg], par.at[4 + 4 * sg, n], across_up, k_up).start()

        @pl.when(first)
        def _():
            copy(x_ref.at[0, 4 - 2 * n * sg], par.at[4 - 4 * sg, n], across_down, k_down).start()

    local = [
        pltpu.make_async_copy(x_ref.at[0, wide], own.at[4, w6], lsem.at[0]),
        pltpu.make_async_copy(x_ref.at[0, far], own.at[4, 6], lsem.at[1]),
    ]
    for c in local:
        c.start()
    near = []
    for dst, slot in ((up, slot_up), (down, slot_down)):
        near.append(send(x_ref.at[0, wide], own.at[slot, w6], dst))
        near.append(send(x_ref.at[0, far], own.at[slot, 6], dst))
    arrive = []
    for o, dst in zip(others, peers):
        slot = 4 + sg * (x - o)
        arrive.append(send(x_ref.at[0, wide], own.at[slot, w6], dst))
        arrive.append(send(x_ref.at[0, far], own.at[slot, 6], dst))
    for c in near:
        c.wait_recv()
    passed = []
    for o, dst in zip(others, peers):
        lower = o < x
        mine = jnp.where(lower, slot_up, slot_down)
        slot = 4 + sg * (x - o + jnp.where(lower, -4, 4))
        passed.append((mine, slot, dst))
        arrive.append(send(own.at[mine], own.at[slot], dst))
    for n in range(3):
        cross[n].wait_recv()
        c_up = copy(par.at[4, n], par.at[slot_up, n], up, edge_up[n])
        c_down = copy(par.at[4, n], par.at[slot_down, n], down, edge_down[n])

        @pl.when(jnp.logical_not(last))
        def _():
            c_up.start()

        @pl.when(jnp.logical_not(first))
        def _():
            c_down.start()

        pending.extend([c_up, c_down])
        for o, dst in zip(others, peers):
            arrive.append(send(par.at[4, n], par.at[4 + sg * (x - o), n], dst))
        c_up.wait_recv()
        c_down.wait_recv()
        for mine, slot, dst in passed:
            arrive.append(send(par.at[mine, n], par.at[slot, n], dst))
    for c in local:
        c.wait()
    for c in arrive:
        c.wait_recv()
    for c in pending:
        c.wait_send()


COPIES = 3 + 6 + 4 + 6 + 3 + 3 * 6


def split(v):
    hi = v.astype(BF16)
    return hi, (v - hi.astype(F32)).astype(BF16)


def dot3(ah, al, bh, bl, dims):
    def d(a, b):
        return lax.dot_general(a, b, dims, preferred_element_type=F32)

    return d(ah, bh) + d(ah, bl) + d(al, bh)


def evaluate(total, reach, own, par, out, xh, xl, sh, sl, nh, nl, rh, rl):
    gr, gc = lax.axis_index("gr"), lax.axis_index("gc")
    s = lax.rem(gc, 2)
    sg = 1 - 2 * s
    row = gr * 8 + gc
    at0 = 1 + 3 * s
    r = [reach[lax.rem(row + sg * (a - 8) + total, total)] for a in range(18)]

    def keep(a, b):
        ok = abs(a - b) <= jnp.minimum(r[a], r[b])
        return jnp.where(ok, 1.0, 0.0).astype(F32)

    def put(a, b, v):
        J, K = a // 2, b // 2
        rows = pl.ds((a % 2) * BS, BS)
        cols = pl.ds((K - J + 2) * G + (b % 2) * BS, BS)
        hi, lo = split(v)
        xh[J, rows, cols] = hi
        xl[J, rows, cols] = lo

    def both(a, b, v):
        if 0 <= b < 18:
            put(a, b, v)
            if a != b:
                put(b, a, v.T)

    zero = jnp.zeros((BS, BS), F32)
    for k in range(9):
        a = 2 * k
        for d in range(-1, 5):
            if d == -1 and k == 0:
                continue
            both(a, a + d, own[k, at0 + sg * d])
        both(a, a - 3, own[k, 6])
        for n in range(3):
            both(a + 1, a + 1 + 2 * n, par[k, n])
        if a + 5 < 18:
            put(a, a + 5, zero)
            put(a + 5, a, zero)

    def span(J, lo, hi):
        return pl.ds((lo - J + 2) * G, (hi - lo + 1) * G)

    def masked(J, K, v):
        return jnp.concatenate(
            [
                jnp.concatenate([v[:BS, :BS] * keep(2 * J, 2 * K), v[:BS, BS:] * keep(2 * J, 2 * K + 1)], axis=1),
                jnp.concatenate([v[BS:, :BS] * keep(2 * J + 1, 2 * K), v[BS:, BS:] * keep(2 * J + 1, 2 * K + 1)], axis=1),
            ],
            axis=0,
        )

    for J in range(2, 7):
        for K in range(J - 2, J + 3):
            lo, hi = max(J, K) - 2, min(J, K) + 2
            a, b = span(J, lo, hi), span(K, lo, hi)
            v = masked(J, K, dot3(xh[J, :, a], xl[J, :, a], xh[K, :, b], xl[K, :, b], NT))
            cols = span(J, K, K)
            sh[J - 2, :, cols], sl[J - 2, :, cols] = split(v)
    for J in range(2, 7):
        for K in range(max(2, J - 2), min(6, J + 2) + 1):
            lo, hi = max(J, K) - 2, min(J, K) + 2
            a, b = span(J, lo, hi), span(K, lo, hi)
            cube = dot3(sh[J - 2, :, a], sl[J - 2, :, a], xh[K, :, b], xl[K, :, b], NT)
            cols = span(J, K, K)
            square = sh[J - 2, :, cols].astype(F32) + sl[J - 2, :, cols].astype(F32)
            hi_, lo_ = split(masked(J, K, 3.0 * square - 2.0 * cube))
            rows = span(K, J, J)
            nh[K - 2, rows, :] = hi_
            nl[K - 2, rows, :] = lo_
            if J == 4:
                rh[:, cols] = hi_[:BS]
                rl[:, cols] = lo_[:BS]
    squares = []
    for K in range(2, 7):
        lo, hi = max(4, K) - 2, min(4, K) + 2
        a, b = span(4, lo, hi), span(K, lo, hi)
        v = dot3(rh[:, a], rl[:, a], nh[K - 2, b, :], nl[K - 2, b, :], NN)
        v = jnp.concatenate([v[:, :BS] * keep(8, 2 * K), v[:, BS:] * keep(8, 2 * K + 1)], axis=1)
        squares.append(v)
    sq = [split(v) for v in squares]
    for K in range(2, 7):
        lo, hi = max(4, K) - 2, min(4, K) + 2
        b = span(K, lo, hi)
        ah = jnp.concatenate([sq[L - 2][0] for L in range(lo, hi + 1)], axis=1)
        al = jnp.concatenate([sq[L - 2][1] for L in range(lo, hi + 1)], axis=1)
        v = 3.0 * squares[K - 2] - 2.0 * dot3(ah, al, nh[K - 2, b, :], nl[K - 2, b, :], NN)
        for h in range(2):
            m = 2 * K + h
            if abs(m - 8) <= 4:
                out[0, 4 + sg * (m - 8)] = v[:, h * BS : (h + 1) * BS] * keep(8, m)


WORK = [
    pltpu.VMEM((9, G, 5 * G), BF16),
    pltpu.VMEM((9, G, 5 * G), BF16),
    pltpu.VMEM((5, G, 5 * G), BF16),
    pltpu.VMEM((5, G, 5 * G), BF16),
    pltpu.VMEM((5, 5 * G, G), BF16),
    pltpu.VMEM((5, 5 * G, G), BF16),
    pltpu.VMEM((BS, 5 * G), BF16),
    pltpu.VMEM((BS, 5 * G), BF16),
]
LAND = [(9, 7, BS, BS), (9, 3, BS, BS)]
SEMS = [pltpu.SemaphoreType.DMA((COPIES,)), pltpu.SemaphoreType.DMA((COPIES,)), pltpu.SemaphoreType.DMA((2,))]
VMEM_LIMIT = 58 << 20
MERGED = True


def solution(mesh):
    lines = mesh.shape["gr"]
    spec = P(("gr", "gc"), None, None, None)

    def local(density, reach):
        total = reach.shape[0]
        out = jax.ShapeDtypeStruct(density.shape, F32)
        smem = pl.BlockSpec(memory_space=pltpu.SMEM)
        vmem = pl.BlockSpec(memory_space=pltpu.VMEM)
        hbm = pl.BlockSpec(memory_space=pl.ANY)
        if MERGED:

            def kernel(reach_ref, x_ref, out_ref, own, par, ssem, rsem, lsem, *work):
                exchange(lines, x_ref, own, par, ssem, rsem, lsem)
                evaluate(total, reach_ref, own, par, out_ref, *work)

            return pl.pallas_call(
                kernel,
                out_shape=out,
                in_specs=[smem, hbm],
                out_specs=vmem,
                scratch_shapes=[pltpu.VMEM(sh, F32) for sh in LAND] + SEMS + WORK,
                compiler_params=pltpu.CompilerParams(collective_id=0, has_side_effects=True, vmem_limit_bytes=VMEM_LIMIT),
            )(reach, density)

        def comm(x_ref, own, par, ssem, rsem, lsem):
            exchange(lines, x_ref, own, par, ssem, rsem, lsem)

        def comp(reach_ref, own, par, out_ref, *work):
            evaluate(total, reach_ref, own, par, out_ref, *work)

        own, par = pl.pallas_call(
            comm,
            out_shape=[jax.ShapeDtypeStruct(sh, F32) for sh in LAND],
            in_specs=[hbm],
            out_specs=[hbm, hbm],
            scratch_shapes=SEMS,
            compiler_params=pltpu.CompilerParams(collective_id=0, has_side_effects=True),
        )(density)
        return pl.pallas_call(
            comp,
            out_shape=out,
            in_specs=[smem, vmem, vmem],
            out_specs=vmem,
            scratch_shapes=WORK,
            compiler_params=pltpu.CompilerParams(vmem_limit_bytes=VMEM_LIMIT),
        )(reach, own, par)

    return jax.shard_map(local, mesh=mesh, in_specs=(spec, P()), out_specs=spec, check_vma=False)
```

time: 873 us -> 125 us (0.14)
  the two profiles are of different devices: /device:TPU:409 before, /device:TPU:2 now
where the time goes in v1:
time: 125 us
  Pallas kernels  123 us (98%)
  local copies, waits for them, and re-layouts  1.92 us (2%)
    pallas_call x1, Pallas kernels, local(): pl.pallas_call(kernel, out_shape=out, in_specs=[smem, hbm], out_specs=vme...  123 us

profile of v1, /device:TPU:2, one launch (start us, length us, event | category | flops | bytes accessed | tf_op | source)
XLA Modules:
  0.0 124.8 jit_solution(15578434349179437037)
XLA Ops:
  0.0 122.9 %shard_map.28 = f32[1,9,128,128]{3,2,1,0:T(8,128)} custom-call(s32[1024]{0:T(1024)} %reach_ref.1, f32[1,9,128,128]{3,2,1,0:T(8,128)} %x_ref.1), custom_call_target="tpu_custom_call" | custom-call | tf_op jit(solution)/shard_map/pallas_call | solution.py:274
  122.9 1.9 %copy.4 = f32[1,9,128,128]{3,2,1,0:T(8,128)} copy(f32[1,9,128,128]{3,2,1,0:T(8,128)} %shard_map.28) | data formatting | bytes 1179648

commit v2 on v1

v2 whole, which is shorter than its diff:
```python
import jax
import jax.numpy as jnp
from jax import lax
from jax.experimental import pallas as pl
from jax.experimental.pallas import tpu as pltpu
from jax.sharding import PartitionSpec as P

MESH = pl.DeviceIdType.MESH
BS = 128
G = 2 * BS
F32 = jnp.float32
BF16 = jnp.bfloat16
NT = (((1,), (1,)), ((), ()))
NN = (((1,), (0,)), ((), ()))


def exchange(lines, x_ref, own, par, ssem, rsem, lsem, meanwhile=lambda: None):
    gr, gc = lax.axis_index("gr"), lax.axis_index("gc")
    x, s = gc // 2, lax.rem(gc, 2)
    sg = 1 - 2 * s
    side = 2 * lax.rem(gr, 2) - 1
    partner_gc = gc + sg
    partner = (gr, partner_gc)
    next_line = lax.rem(gr + side + lines, lines)
    out = (next_line, gc)
    mate = (gr - side, gc)
    steps = (1, 3, 2)
    others = [lax.rem(x + step, 4) for step in steps]
    peers = [(gr, o * 2 + s) for o in others]

    own_wide = pltpu.make_async_copy(x_ref.at[0, pl.ds(3 - 3 * s, 6)], own.at[4, pl.ds(0, 6)], lsem.at[0])
    own_far = pltpu.make_async_copy(x_ref.at[0, 4 - 3 * sg], own.at[4, 6], lsem.at[1])
    own_wide.start()
    own_far.start()

    barrier = pltpu.get_barrier_semaphore()
    pair, pairs = gr * 4 + x, lines * 4
    around, extra = [], 0
    for k in HOPS:
        q = pair + k
        wraps = jnp.logical_or(q < 0, q >= pairs)
        q = lax.rem(q + pairs, pairs)
        same = (q // 4, lax.rem(q, 4) * 2 + s)
        flipped = (same[0], same[1] + sg)
        around.append((k, wraps, same, flipped))
        extra = extra + jnp.where(wraps, 1, 0)
    for d in [partner] + [a[2] for a in around]:
        pl.semaphore_signal(barrier, inc=1, device_id=d, device_id_type=MESH)
    for _, wraps, _, flipped in around:

        @pl.when(wraps)
        def _(flipped=flipped):
            pl.semaphore_signal(barrier, inc=1, device_id=flipped, device_id_type=MESH)

    own_wide.wait()
    own_far.wait()
    pl.semaphore_wait(barrier, 1 + len(HOPS) + extra)

    pending = []

    def copy(src, dst, device, k, arrives=None):
        c = pltpu.make_async_remote_copy(
            src, dst, ssem.at[k], rsem.at[k if arrives is None else arrives], device_id=device, device_id_type=MESH
        )
        pending.append(c)
        return c

    slot_out, slot_back = 4 + 4 * sg * side, 4 - 4 * sg * side

    def routes(buffer, base, pick):
        def at(slot):
            return pick(buffer, slot)

        here = at(4)
        near = [copy(here, at(slot_back), out, base), copy(here, at(slot_out), mate, base + 1)]
        line, onward = [], []
        for j, (step, o, dst) in enumerate(zip(steps, others, peers)):
            line.append(copy(here, at(4 + sg * (x - o)), dst, base + 2 + j, base + 2 + (1, 0, 2)[j]))
            to_peer = (o - x) * side > 0
            src = jnp.where(to_peer, slot_out, 4 + sg * (o - x))
            k = jnp.where(to_peer, x - o, o - x)
            dst_slot = 4 + sg * (k + 4 * side)
            device = (jnp.where(to_peer, dst[0], mate[0]), jnp.where(to_peer, dst[1], mate[1]))
            arrives = base + 5 + jnp.where(to_peer, (1, 0, 2)[j], j)
            onward.append((to_peer, copy(at(src), at(dst_slot), device, base + 5 + j, arrives)))
        return near, line, onward

    def arrived(j, base, piece):
        return pltpu.make_async_remote_copy(
            piece, piece, ssem.at[base + 5 + j], rsem.at[base + 5 + j], device_id=mate, device_id_type=MESH
        )

    def start_if(cond, c):
        @pl.when(cond)
        def _():
            c.start()

    early = [routes(own, 5 + 8 * e, lambda ref, slot, p=p: ref.at[slot, p]) for e, p in enumerate(PIECES)]
    base = 5 + 8 * len(PIECES)
    cross = [
        copy(x_ref.at[(0, 4 - 2 * q[0] * sg) + q[1:]], par.at[(4,) + q], partner, n) for n, q in enumerate(PARTS)
    ]
    hot = (next_line // 8) != (gr // 8)

    for near, _, _ in early:
        near[0].start()
    for c in cross:
        c.start()
    late = []
    for n, q in enumerate(PARTS):
        copies = []
        for j, (k, wraps, same, flipped) in enumerate(around):
            sem, there = base + 8 * n + j, base + 8 * n + (j ^ 1)
            c = copy(par.at[(4,) + q], par.at[(4 - sg * k,) + q], same, sem, there)
            copies.append((wraps, c))
            own_row = pltpu.make_async_remote_copy(
                x_ref.at[(0, 4 - 2 * q[0] * sg) + q[1:]],
                par.at[(4 + sg * k,) + q],
                ssem.at[sem],
                rsem.at[there],
                device_id=flipped,
                device_id_type=MESH,
            )
            start_if(wraps, own_row)
        late.append(copies)
    for _, line, _ in early:
        for c in line:
            c.start()
    for near, _, _ in early:
        near[1].start()

    def pass_out(route):
        near, _, onward = route
        near[0].wait_recv()
        for to_peer, c in onward:
            start_if(to_peer, c)

    def pass_mate(route):
        _, line, onward = route
        for j, (to_peer, c) in enumerate(onward):
            line[(1, 0, 2)[j]].wait_recv()
            start_if(jnp.logical_not(to_peer), c)

    def spread(n):
        cross[n].wait_recv()
        for wraps, c in late[n]:
            start_if(jnp.logical_not(wraps), c)

    for route in early:
        pass_mate(route)
    spread(0)

    @pl.when(jnp.logical_not(hot))
    def _():
        for route in early:
            pass_out(route)

    for n in range(1, len(PARTS)):
        spread(n)

    @pl.when(hot)
    def _():
        for route in early:
            pass_out(route)

    for e, p in enumerate(PIECES):
        early[e][0][1].wait_recv()
        for j in range(3):
            arrived(j, 5 + 8 * e, own.at[4, p]).wait_recv()
    meanwhile()
    for copies in late:
        for _, c in copies:
            c.wait_recv()
    for c in pending:
        c.wait_send()


HOPS = (4, -4, 3, -3, 2, -2, 1, -1)
PIECES = (pl.ds(0, 7),)
PARTS = ((0,), (1,), (2,))
COPIES = 5 + 8 * len(PIECES) + 8 * len(PARTS)


def split(v):
    hi = v.astype(BF16)
    return hi, (v - hi.astype(F32)).astype(BF16)


def dot3(ah, al, bh, bl, dims):
    def d(a, b):
        return lax.dot_general(a, b, dims, preferred_element_type=F32)

    return d(ah, bh) + d(ah, bl) + d(al, bh)


def evaluate(total, reach, own, par, out, xh, xl, sh, sl, nh, nl, rh, rl, between=None):
    gr, gc = lax.axis_index("gr"), lax.axis_index("gc")
    s = lax.rem(gc, 2)
    sg = 1 - 2 * s
    row = gr * 8 + gc
    at0 = 1 + 3 * s
    r = [reach[lax.rem(row + sg * (a - 8) + total, total)] for a in range(18)]

    def keep(a, b):
        ok = abs(a - b) <= jnp.minimum(r[a], r[b])
        return jnp.where(ok, 1.0, 0.0).astype(F32)

    def put(a, b, v):
        J, K = a // 2, b // 2
        rows = pl.ds((a % 2) * BS, BS)
        cols = pl.ds((K - J + 2) * G + (b % 2) * BS, BS)
        hi, lo = split(v)
        xh[J, rows, cols] = hi
        xl[J, rows, cols] = lo

    def both(a, b, v):
        if 0 <= b < 18:
            put(a, b, v)
            if a != b:
                put(b, a, v.T)

    zero = jnp.zeros((BS, BS), F32)

    def rows_here(k):
        a = 2 * k
        for d in range(-1, 5):
            if d == -1 and k == 0:
                continue
            both(a, a + d, own[k, at0 + sg * d])
        both(a, a - 3, own[k, 6])
        if a + 5 < 18:
            put(a, a + 5, zero)
            put(a + 5, a, zero)

    def all_here():
        for k in range(9):
            rows_here(k)

    if between is None:
        all_here()
    else:
        between(all_here)
    for k in range(9):
        for n in range(3):
            both(2 * k + 1, 2 * k + 1 + 2 * n, par[k, n])

    def span(J, lo, hi):
        return pl.ds((lo - J + 2) * G, (hi - lo + 1) * G)

    def masked(J, K, v):
        return jnp.concatenate(
            [
                jnp.concatenate([v[:BS, :BS] * keep(2 * J, 2 * K), v[:BS, BS:] * keep(2 * J, 2 * K + 1)], axis=1),
                jnp.concatenate([v[BS:, :BS] * keep(2 * J + 1, 2 * K), v[BS:, BS:] * keep(2 * J + 1, 2 * K + 1)], axis=1),
            ],
            axis=0,
        )

    for J in range(2, 7):
        for K in range(J - 2, J + 3):
            if 2 <= K < J:
                continue
            lo, hi = max(J, K) - 2, min(J, K) + 2
            a, b = span(J, lo, hi), span(K, lo, hi)
            v = masked(J, K, dot3(xh[J, :, a], xl[J, :, a], xh[K, :, b], xl[K, :, b], NT))
            cols = span(J, K, K)
            sh[J - 2, :, cols], sl[J - 2, :, cols] = split(v)
            if J < K < 7:
                cols = span(K, J, J)
                sh[K - 2, :, cols], sl[K - 2, :, cols] = split(v.T)
    for J in range(2, 7):
        for K in range(max(2, J - 2), min(6, J + 2) + 1):
            lo, hi = max(J, K) - 2, min(J, K) + 2
            a, b = span(J, lo, hi), span(K, lo, hi)
            cube = dot3(sh[J - 2, :, a], sl[J - 2, :, a], xh[K, :, b], xl[K, :, b], NT)
            cols = span(J, K, K)
            square = sh[J - 2, :, cols].astype(F32) + sl[J - 2, :, cols].astype(F32)
            hi_, lo_ = split(masked(J, K, 3.0 * square - 2.0 * cube))
            rows = span(K, J, J)
            nh[K - 2, rows, :] = hi_
            nl[K - 2, rows, :] = lo_
            if J == 4:
                rh[:, cols] = hi_[:BS]
                rl[:, cols] = lo_[:BS]
    squares = []
    for K in range(2, 7):
        lo, hi = max(4, K) - 2, min(4, K) + 2
        a, b = span(4, lo, hi), span(K, lo, hi)
        v = dot3(rh[:, a], rl[:, a], nh[K - 2, b, :], nl[K - 2, b, :], NN)
        v = jnp.concatenate([v[:, :BS] * keep(8, 2 * K), v[:, BS:] * keep(8, 2 * K + 1)], axis=1)
        squares.append(v)
    sq = [split(v) for v in squares]
    for K in range(2, 7):
        lo, hi = max(4, K) - 2, min(4, K) + 2
        b = span(K, lo, hi)
        ah = jnp.concatenate([sq[L - 2][0] for L in range(lo, hi + 1)], axis=1)
        al = jnp.concatenate([sq[L - 2][1] for L in range(lo, hi + 1)], axis=1)
        v = 3.0 * squares[K - 2] - 2.0 * dot3(ah, al, nh[K - 2, b, :], nl[K - 2, b, :], NN)
        for h in range(2):
            m = 2 * K + h
            if abs(m - 8) <= 4:
                out[0, 4 + sg * (m - 8)] = v[:, h * BS : (h + 1) * BS] * keep(8, m)


WORK = [
    pltpu.VMEM((9, G, 5 * G), BF16),
    pltpu.VMEM((9, G, 5 * G), BF16),
    pltpu.VMEM((5, G, 5 * G), BF16),
    pltpu.VMEM((5, G, 5 * G), BF16),
    pltpu.VMEM((5, 5 * G, G), BF16),
    pltpu.VMEM((5, 5 * G, G), BF16),
    pltpu.VMEM((BS, 5 * G), BF16),
    pltpu.VMEM((BS, 5 * G), BF16),
]
LAND = [(9, 7, BS, BS), (9, 3, BS, BS)]
SEMS = [pltpu.SemaphoreType.DMA((COPIES,)), pltpu.SemaphoreType.DMA((COPIES,)), pltpu.SemaphoreType.DMA((2,))]
VMEM_LIMIT = 58 << 20


def solution(mesh):
    lines = mesh.shape["gr"]
    spec = P(("gr", "gc"), None, None, None)

    def local(density, reach):
        total = reach.shape[0]

        def kernel(reach_ref, x_ref, out_ref, own, par, ssem, rsem, lsem, *work):
            def between(meanwhile):
                exchange(lines, x_ref, own, par, ssem, rsem, lsem, meanwhile)

            evaluate(total, reach_ref, own, par, out_ref, *work, between=between)

        return pl.pallas_call(
            kernel,
            out_shape=jax.ShapeDtypeStruct(density.shape, F32),
            in_specs=[pl.BlockSpec(memory_space=pltpu.SMEM), pl.BlockSpec(memory_space=pl.ANY)],
            out_specs=pl.BlockSpec(memory_space=pltpu.VMEM),
            scratch_shapes=[pltpu.VMEM(shape, F32) for shape in LAND] + SEMS + WORK,
            compiler_params=pltpu.CompilerParams(collective_id=0, has_side_effects=True, vmem_limit_bytes=VMEM_LIMIT),
        )(reach, density)

    return jax.shard_map(local, mesh=mesh, in_specs=(spec, P()), out_specs=spec, check_vma=False)
```

time: 125 us -> 119 us (0.952)
  Pallas kernels: 123 us -> 117 us
    pallas_call x1, Pallas kernels: 123 us -> 117 us  [local(): pl.pallas_call(kernel, out_shape=jax.ShapeDtypeStruct(density.shape, F32)...]
where the time goes in v2:
time: 119 us
  Pallas kernels  117 us (98%)
  local copies, waits for them, and re-layouts  1.92 us (2%)
    pallas_call x1, Pallas kernels, local(): pl.pallas_call(kernel, out_shape=jax.ShapeDtypeStruct(density.shape, F32)...  117 us

profile of v2, /device:TPU:2, one launch (start us, length us, event | category | flops | bytes accessed | tf_op | source)
XLA Modules:
  0.0 118.9 jit_solution(3986126699410227920)
XLA Ops:
  0.0 117.0 %shard_map.28 = f32[1,9,128,128]{3,2,1,0:T(8,128)} custom-call(s32[1024]{0:T(1024)} %reach_ref.1, f32[1,9,128,128]{3,2,1,0:T(8,128)} %x_ref.1), custom_call_target="tpu_custom_call" | custom-call | tf_op jit(solution)/shard_map/pallas_call | solution.py:333
  117.0 1.9 %copy.4 = f32[1,9,128,128]{3,2,1,0:T(8,128)} copy(f32[1,9,128,128]{3,2,1,0:T(8,128)} %shard_map.28) | data formatting | bytes 1179648

commit v3 on v2

--- a/solution.py
+++ b/solution.py
@@ -8,13 +8,40 @@
 MESH = pl.DeviceIdType.MESH
 BS = 128
 G = 2 * BS
+HB = BS // 2
 F32 = jnp.float32
 BF16 = jnp.bfloat16
 NT = (((1,), (1,)), ((), ()))
 NN = (((1,), (0,)), ((), ()))
 
 
-def exchange(lines, x_ref, own, par, ssem, rsem, lsem, meanwhile=lambda: None):
+def triangles():
+    r = lax.broadcasted_iota(jnp.int32, (HB, HB), 0)
+    c = lax.broadcasted_iota(jnp.int32, (HB, HB), 1)
+    return r, c
+
+
+def pack(v):
+    r, c = triangles()
+    low = v[HB:, HB:]
+    both = jnp.where(r <= c, v[:HB, :HB], low)
+    diagonal = jnp.sum(jnp.where(r == c, low, 0.0), axis=0, keepdims=True)
+    tail = jnp.concatenate([diagonal, jnp.zeros((1, HB), F32)], axis=1)
+    return jnp.concatenate([both, v[:HB, HB:]], axis=1), jnp.broadcast_to(tail, (8, BS))
+
+
+def unpack(top, tail):
+    r, c = triangles()
+    both, corner = top[:, :HB], top[:, HB:]
+    turned = both.T
+    high = jnp.where(r <= c, both, turned)
+    low = jnp.where(r > c, both, jnp.where(r < c, turned, jnp.broadcast_to(tail[:1, :HB], (HB, HB))))
+    return jnp.concatenate(
+        [jnp.concatenate([high, corner], axis=1), jnp.concatenate([corner.T, low], axis=1)], axis=0
+    )
+
+
+def exchange(lines, x_ref, own, par, packed, ssem, rsem, lsem, meanwhile=lambda: None):
     gr, gc = lax.axis_index("gr"), lax.axis_index("gc")
     x, s = gc // 2, lax.rem(gc, 2)
     sg = 1 - 2 * s
@@ -54,6 +81,7 @@
 
     own_wide.wait()
     own_far.wait()
+    packed[pl.ds(0, HB), :], packed[pl.ds(HB, 8), :] = pack(own[4, 1 + 3 * s])
     pl.semaphore_wait(barrier, 1 + len(HOPS) + extra)
 
     pending = []
@@ -97,9 +125,8 @@
 
     early = [routes(own, 5 + 8 * e, lambda ref, slot, p=p: ref.at[slot, p]) for e, p in enumerate(PIECES)]
     base = 5 + 8 * len(PIECES)
-    cross = [
-        copy(x_ref.at[(0, 4 - 2 * q[0] * sg) + q[1:]], par.at[(4,) + q], partner, n) for n, q in enumerate(PARTS)
-    ]
+    mine = [packed if n == 0 else x_ref.at[(0, 4 - 2 * q[0] * sg) + q[1:]] for n, q in enumerate(PARTS)]
+    cross = [copy(mine[n], par.at[(4,) + q], partner, n) for n, q in enumerate(PARTS)]
     hot = (next_line // 8) != (gr // 8)
 
     for near, _, _ in early:
@@ -114,7 +141,7 @@
             c = copy(par.at[(4,) + q], par.at[(4 - sg * k,) + q], same, sem, there)
             copies.append((wraps, c))
             own_row = pltpu.make_async_remote_copy(
-                x_ref.at[(0, 4 - 2 * q[0] * sg) + q[1:]],
+                mine[n],
                 par.at[(4 + sg * k,) + q],
                 ssem.at[sem],
                 rsem.at[there],
@@ -177,7 +204,7 @@
 
 HOPS = (4, -4, 3, -3, 2, -2, 1, -1)
 PIECES = (pl.ds(0, 7),)
-PARTS = ((0,), (1,), (2,))
+PARTS = ((0, pl.ds(0, 72)), (1,), (2,))
 COPIES = 5 + 8 * len(PIECES) + 8 * len(PARTS)
 
 
@@ -241,7 +268,8 @@
     else:
         between(all_here)
     for k in range(9):
-        for n in range(3):
+        put(2 * k + 1, 2 * k + 1, unpack(par[k, 0, pl.ds(0, HB), :], par[k, 0, pl.ds(HB, 8), :]))
+        for n in (1, 2):
             both(2 * k + 1, 2 * k + 1 + 2 * n, par[k, n])
 
     def span(J, lo, hi):
@@ -324,9 +352,9 @@
     def local(density, reach):
         total = reach.shape[0]
 
-        def kernel(reach_ref, x_ref, out_ref, own, par, ssem, rsem, lsem, *work):
+        def kernel(reach_ref, x_ref, out_ref, own, par, packed, ssem, rsem, lsem, *work):
             def between(meanwhile):
-                exchange(lines, x_ref, own, par, ssem, rsem, lsem, meanwhile)
+                exchange(lines, x_ref, own, par, packed, ssem, rsem, lsem, meanwhile)
 
             evaluate(total, reach_ref, own, par, out_ref, *work, between=between)
 
@@ -335,7 +363,7 @@
             out_shape=jax.ShapeDtypeStruct(density.shape, F32),
             in_specs=[pl.BlockSpec(memory_space=pltpu.SMEM), pl.BlockSpec(memory_space=pl.ANY)],
             out_specs=pl.BlockSpec(memory_space=pltpu.VMEM),
-            scratch_shapes=[pltpu.VMEM(shape, F32) for shape in LAND] + SEMS + WORK,
+            scratch_shapes=[pltpu.VMEM(shape, F32) for shape in LAND] + [pltpu.VMEM((72, BS), F32)] + SEMS + WORK,
             compiler_params=pltpu.CompilerParams(collective_id=0, has_side_effects=True, vmem_limit_bytes=VMEM_LIMIT),
         )(reach, density)
 

time: 119 us -> 113 us (0.950)
  Pallas kernels: 117 us -> 110 us
    pallas_call x1, Pallas kernels: 117 us -> 110 us  [local(): pl.pallas_call(kernel, out_shape=jax.ShapeDtypeStruct(density.shape, F32)...]
where the time goes in v3:
time: 113 us; the launch traced here: 112 us
  Pallas kernels  110 us (97%)
  local copies, waits for them, and re-layouts  1.92 us (2%)
    pallas_call x1, Pallas kernels, local(): pl.pallas_call(kernel, out_shape=jax.ShapeDtypeStruct(density.shape, F32)...  110 us

profile of v3, /device:TPU:2, one launch (start us, length us, event | category | flops | bytes accessed | tf_op | source)
XLA Modules:
  0.0 112.4 jit_solution(6333324472230450240)
XLA Ops:
  0.0 110.5 %shard_map.28 = f32[1,9,128,128]{3,2,1,0:T(8,128)} custom-call(s32[1024]{0:T(1024)} %reach_ref.1, f32[1,9,128,128]{3,2,1,0:T(8,128)} %x_ref.1), custom_call_target="tpu_custom_call" | custom-call | tf_op jit(solution)/shard_map/pallas_call | solution.py:361
  110.5 1.9 %copy.4 = f32[1,9,128,128]{3,2,1,0:T(8,128)} copy(f32[1,9,128,128]{3,2,1,0:T(8,128)} %shard_map.28) | data formatting | bytes 1179648
